TPU v7x, 32 devices: a whole 2x2x4 slice. The times are simulated.
32 devices in a mesh: groups: 1, seq: 32 (over z, y, x, core), tp: 1.
Axes of the slice: x: 2, y: 2, z: 4, core: 2. Of those that a mesh axis runs over, the one named last changes fastest.
Arguments:
- resid: bfloat16 [6144, 3584], P(('groups', 'seq')), may hold values from -14 to 14
- gate_pre: bfloat16 [6144, 9472], P(('groups', 'seq'), 'tp'), may hold values from -6 to 6
- up_pre: bfloat16 [6144, 9472], P(('groups', 'seq'), 'tp'), may hold values from -6 to 6
- down_weight: bfloat16 [9472, 3584], P(('tp', 'seq')), may hold values from -0.0625 to 0.0625
- norm_gain: float32 [3584], replicated, may hold values from 0.1 to 1.9
- value_head: float32 [3584], replicated, may hold values from -0.09375 to 0.09375
- rewards: float32 [6144], P(('groups', 'seq')), may hold values from -0.12 to 0.12
- seg_ids: int32 [6144], P(('groups', 'seq')), may hold values from 0 to 7, never falling along the last dimension, each value on 1 to 1536 neighbouring positions
Outputs:
- values: float32 [6144], P(('groups', 'seq'))
- advantages: float32 [6144], P(('groups', 'seq'))
- grad_gate: bfloat16 [6144, 9472], P(('groups', 'seq'), 'tp')
- grad_up: bfloat16 [6144, 9472], P(('groups', 'seq'), 'tp')
- grad_resid: bfloat16 [6144, 3584], P(('groups', 'seq'))
Inputs may be any that keep to these rules, and one draw needn't show every extreme that they name: `seg_ids`: never falls along the stream; each document holds 1 to 1536 tokens, one exactly 1536.
All inputs are finite; a program needn't handle non-finite values.
Results may differ from a plain program's by a relative error of at most 0.00225.
The roundings to bfloat16 on the way count: a program that leaves them out, or rounds other values in their place, can miss the bound.
Values may be sent and summed in bfloat16 or wider, within the bound.
A program may use at most 192 MiB of HBM per device.

v0:
```python
import jax
import jax.numpy as jnp
from jax import lax
from jax.sharding import PartitionSpec as P

D = 3584


EPS = 1e-06


def from_behind(shard, axis, by):
    length = lax.axis_size(axis)
    pairs = [(i, i + by) for i in range(length) if 0 <= i + by < length]
    return lax.ppermute(shard, axis, pairs)


def combine_runs(right, left):
    left_first, left_last, left_total = left
    right_first, right_last, right_total = right
    joined = jnp.logical_and(left_first == left_last, left_last == right_first)
    merged_total = left_total + jnp.where(joined, right_total, 0.0)
    merged_last = jnp.where(right_first > 0.0, right_last, left_last)
    left_empty = left_first <= 0.0
    return (
        jnp.where(left_empty, right_first, left_first),
        jnp.where(left_empty, right_last, merged_last),
        jnp.where(left_empty, right_total, merged_total),
    )


def doc_returns(rewards, seg_ids):
    count = rewards.shape[0]
    places = lax.broadcasted_iota(jnp.int32, (count, count), 0)
    others = lax.broadcasted_iota(jnp.int32, (count, count), 1)
    same_doc = seg_ids[:, None] == seg_ids[None, :]
    suffix = jnp.where(jnp.logical_and(same_doc, others >= places), 1.0, 0.0).astype(jnp.float32)
    local_sum = jnp.dot(suffix, rewards, precision=lax.Precision.HIGHEST)
    first_id = seg_ids[0]
    last_id = seg_ids[count - 1]
    first_total = jnp.sum(jnp.where(seg_ids == first_id, rewards, 0.0))
    own = (
        (first_id + 1).astype(jnp.float32).reshape(1),
        (last_id + 1).astype(jnp.float32).reshape(1),
        first_total.reshape(1),
    )
    blank = (
        jnp.zeros((1,), jnp.float32),
        jnp.zeros((1,), jnp.float32),
        jnp.zeros((1,), jnp.float32),
    )

    def advance(step, state):
        sending = combine_runs(state, own)
        return from_behind((sending[0], sending[1], sending[2]), "seq", -1)

    beyond = lax.fori_loop(0, lax.axis_size("seq") - 1, advance, blank)
    last_code = (last_id + 1).astype(jnp.float32)
    carried = jnp.where(beyond[0][0] == last_code, beyond[2][0], 0.0)
    return local_sum + jnp.where(seg_ids == last_id, carried, 0.0)


def body(resid, gate_pre, up_pre, down_weight, norm_gain, value_head, rewards, seg_ids):
    gate = gate_pre.astype(jnp.float32)
    upval = up_pre.astype(jnp.float32)
    sigma = jax.nn.sigmoid(gate)
    active = gate * sigma
    hidden = (active * upval).astype(jnp.bfloat16)
    down_full = lax.all_gather(down_weight, "seq", axis=0, tiled=True)
    partial_value = jnp.dot(hidden, down_full, preferred_element_type=jnp.float32)
    head = norm_gain * value_head
    returns = doc_returns(rewards, seg_ids)
    stream = resid.astype(jnp.float32) + lax.psum(partial_value, "tp")
    rinv = lax.rsqrt(jnp.mean(stream * stream, axis=1) + EPS)
    values = jnp.sum(stream * head[None, :], axis=1) * rinv
    grad_value = 64.0 * (values - returns)
    grad_stream = (grad_value * rinv)[:, None] * (
        head[None, :] - stream * (rinv * values / D)[:, None]
    )
    grad_resid = grad_stream.astype(jnp.bfloat16)
    grad_hidden = lax.dot_general(
        grad_resid, down_full, (((1,), (1,)), ((), ())), preferred_element_type=jnp.float32
    )
    grad_gate = (grad_hidden * upval * sigma * (1.0 + gate * (1.0 - sigma))).astype(jnp.bfloat16)
    grad_up = (grad_hidden * active).astype(jnp.bfloat16)
    advantages = returns - values
    return (values, advantages, grad_gate, grad_up, grad_resid)


def solution(mesh):
    return jax.shard_map(
        body,
        mesh=mesh,
        in_specs=(
            P(("groups", "seq"), None),
            P(("groups", "seq"), "tp"),
            P(("groups", "seq"), "tp"),
            P(("tp", "seq"), None),
            P(),
            P(),
            P(("groups", "seq")),
            P(("groups", "seq")),
        ),
        out_specs=(
            P(("groups", "seq")),
            P(("groups", "seq")),
            P(("groups", "seq"), "tp"),
            P(("groups", "seq"), "tp"),
            P(("groups", "seq"), None),
        ),
        check_vma=False,
    )
```

profile of v0, /device:TPU:15, one launch (start us, length us, event | category | flops | bytes accessed | tf_op | source)
XLA Modules:
  0.0 502.5 jit_solution(4327831055961287293)
XLA Ops:
  12.5 418.2 %while.13 = (s32[]{:T(128)}, f32[1]{0:T(128)}, f32[1]{0:T(128)}, pred[1]{0:T(512)(128)(4,1)}, f32[1]{0:T(128)}, /*index=5*/f32[1]{0:T(128)}, pred[1]{0:T(512)(128)(4,1)}, f32[1]{0:T(128)}, s32[]{:T(128)}, f32[1]{0:T(128)}) while((s32[]{:T(128)}, f32[1]{0:T(128)}, f32[1]{0:T(128)}, pred[1]{0:T(512)(128)(4,1)}, f32[1]{0:T(128)}, ...), condition=%wide.region_4.5_spmd, body=%wide.region_3.4_spmd.sunk | while | flops 8 | bytes 276 | solution.py:57
  13.0 3.5 collective-permute-start.1
  19.7 3.7 collective-permute-done
  32.0 3.9 collective-permute-done
  44.4 3.3 collective-permute-done
  56.3 3.3 collective-permute-done
  80.1 4.0 collective-permute-done
  92.6 6.8 %collective-permute-done = f32[1]{0:T(128)} collective-permute-done((f32[1]{0:T(128)}, f32[1]{0:T(128)}, u32[]{:S(2)}, u32[]{:S(2)}) %collective-permute-start) | collective-permute-done | bytes 36 | tf_op jit(solution)/shard_map/while/body/eval_jaxpr/ppermute | solution.py:15
  107.9 6.7 %collective-permute-done = f32[1]{0:T(128)} collective-permute-done((f32[1]{0:T(128)}, f32[1]{0:T(128)}, u32[]{:S(2)}, u32[]{:S(2)}) %collective-permute-start) | collective-permute-done | bytes 36 | tf_op jit(solution)/shard_map/while/body/eval_jaxpr/ppermute | solution.py:15
  123.1 6.7 %collective-permute-done = f32[1]{0:T(128)} collective-permute-done((f32[1]{0:T(128)}, f32[1]{0:T(128)}, u32[]{:S(2)}, u32[]{:S(2)}) %collective-permute-start) | collective-permute-done | bytes 36 | tf_op jit(solution)/shard_map/while/body/eval_jaxpr/ppermute | solution.py:15
  150.3 4.3 collective-permute-done
  197.7 6.2 %collective-permute-done.1 = f32[1]{0:T(128)} collective-permute-done((f32[1]{0:T(128)}, f32[1]{0:T(128)}, u32[]{:S(2)}, u32[]{:S(2)}) %collective-permute-start.1) | collective-permute-done | bytes 36 | tf_op jit(solution)/shard_map/while/body/eval_jaxpr/ppermute | solution.py:15
  211.5 7.6 %collective-permute-done.1 = f32[1]{0:T(128)} collective-permute-done((f32[1]{0:T(128)}, f32[1]{0:T(128)}, u32[]{:S(2)}, u32[]{:S(2)}) %collective-permute-start.1) | collective-permute-done | bytes 36 | tf_op jit(solution)/shard_map/while/body/eval_jaxpr/ppermute | solution.py:15
  226.8 7.6 %collective-permute-done.1 = f32[1]{0:T(128)} collective-permute-done((f32[1]{0:T(128)}, f32[1]{0:T(128)}, u32[]{:S(2)}, u32[]{:S(2)}) %collective-permute-start.1) | collective-permute-done | bytes 36 | tf_op jit(solution)/shard_map/while/body/eval_jaxpr/ppermute | solution.py:15
  242.0 7.5 %collective-permute-done.1 = f32[1]{0:T(128)} collective-permute-done((f32[1]{0:T(128)}, f32[1]{0:T(128)}, u32[]{:S(2)}, u32[]{:S(2)}) %collective-permute-start.1) | collective-permute-done | bytes 36 | tf_op jit(solution)/shard_map/while/body/eval_jaxpr/ppermute | solution.py:15
  257.1 7.7 %collective-permute-done.1 = f32[1]{0:T(128)} collective-permute-done((f32[1]{0:T(128)}, f32[1]{0:T(128)}, u32[]{:S(2)}, u32[]{:S(2)}) %collective-permute-start.1) | collective-permute-done | bytes 36 | tf_op jit(solution)/shard_map/while/body/eval_jaxpr/ppermute | solution.py:15
  272.4 7.7 %collective-permute-done.1 = f32[1]{0:T(128)} collective-permute-done((f32[1]{0:T(128)}, f32[1]{0:T(128)}, u32[]{:S(2)}, u32[]{:S(2)}) %collective-permute-start.1) | collective-permute-done | bytes 36 | tf_op jit(solution)/shard_map/while/body/eval_jaxpr/ppermute | solution.py:15
  287.6 7.6 %collective-permute-done.1 = f32[1]{0:T(128)} collective-permute-done((f32[1]{0:T(128)}, f32[1]{0:T(128)}, u32[]{:S(2)}, u32[]{:S(2)}) %collective-permute-start.1) | collective-permute-done | bytes 36 | tf_op jit(solution)/shard_map/while/body/eval_jaxpr/ppermute | solution.py:15
  303.8 8.6 %collective-permute-done = f32[1]{0:T(128)} collective-permute-done((f32[1]{0:T(128)}, f32[1]{0:T(128)}, u32[]{:S(2)}, u32[]{:S(2)}) %collective-permute-start) | collective-permute-done | bytes 36 | tf_op jit(solution)/shard_map/while/body/eval_jaxpr/ppermute | solution.py:15
  321.1 6.6 %collective-permute-done = f32[1]{0:T(128)} collective-permute-done((f32[1]{0:T(128)}, f32[1]{0:T(128)}, u32[]{:S(2)}, u32[]{:S(2)}) %collective-permute-start) | collective-permute-done | bytes 36 | tf_op jit(solution)/shard_map/while/body/eval_jaxpr/ppermute | solution.py:15
  336.3 6.6 %collective-permute-done = f32[1]{0:T(128)} collective-permute-done((f32[1]{0:T(128)}, f32[1]{0:T(128)}, u32[]{:S(2)}, u32[]{:S(2)}) %collective-permute-start) | collective-permute-done | bytes 36 | tf_op jit(solution)/shard_map/while/body/eval_jaxpr/ppermute | solution.py:15
  351.6 6.5 %collective-permute-done = f32[1]{0:T(128)} collective-permute-done((f32[1]{0:T(128)}, f32[1]{0:T(128)}, u32[]{:S(2)}, u32[]{:S(2)}) %collective-permute-start) | collective-permute-done | bytes 36 | tf_op jit(solution)/shard_map/while/body/eval_jaxpr/ppermute | solution.py:15
  432.6 28.1 %multiply_reduce_fusion = (f32[192]{0:T(256)S(1)}, f32[192]{0:T(256)S(1)}, f32[192,3584]{1,0:T(8,128)S(1)}) fusion(f32[3584]{0:T(1024)S(1)} %mul.76, bf16[9472,3584]{1,0:T(8,128)(2,1)} %all-gather.2.cloned.1.call-done, bf16[192,9472]{1,0:T(8,128)(2,1)} %param.12, bf16[192,9472]{1,0:T(8,128)(2,1)} %param.11, bf16[192,3584]{1,0:T(8,128)(2,1)} %param.10), kind=kOutput, calls=%fused_computation.16 | convolution fusion | flops 13054574592 | bytes 79314432 | tf_op jit(solution)/shard_map/dot_general | solution.py:70
  463.1 32.6 %multiply_convert_fusion = (bf16[192,9472]{1,0:T(8,128)(2,1)}, bf16[192,9472]{1,0:T(8,128)(2,1)}) fusion(bf16[192,9472]{1,0:T(8,128)(2,1)} %param.11, bf16[192,9472]{1,0:T(8,128)(2,1)} %param.12, bf16[192,3584]{1,0:T(8,128)(2,1)S(1)} %multiply_convert_fusion.1, bf16[9472,3584]{1,0:T(8,128)(2,1)} %all-gather.2.cloned.1.call-done), kind=kOutput, calls=%fused_computation.13 | convolution fusion | flops 13063176192 | bytes 83820544 | tf_op jit(solution)/shard_map/dot_general | solution.py:81
  (119 shorter events, 240.4 us)
Async XLA Ops:
  7.2 425.4 %all-gather.2.cloned.1.call-start = ((), (), s32[]{:S(2)}) async-start(), calls=%async_computation | async-start | bytes 70017024 | tf_op jit(solution)/shard_map/all_gather | solution.py:69
  88.8 10.5 %collective-permute-start = (f32[1]{0:T(128)}, f32[1]{0:T(128)}, u32[]{:S(2)}, u32[]{:S(2)}) collective-permute-start(f32[1]{0:T(128)} %select_n.49), channel_id=1, source_target_pairs={{1,0},{2,1},{3,2},{4,3},{5,4},{6,5},{7,6},{8,7},{9,8},{10,9},{11,1... | collective-permute-start | bytes 20 | tf_op jit(solution)/shard_map/while/body/eval_jaxpr/ppermute | solution.py:15
  104.1 10.5 %collective-permute-start = (f32[1]{0:T(128)}, f32[1]{0:T(128)}, u32[]{:S(2)}, u32[]{:S(2)}) collective-permute-start(f32[1]{0:T(128)} %select_n.49), channel_id=1, source_target_pairs={{1,0},{2,1},{3,2},{4,3},{5,4},{6,5},{7,6},{8,7},{9,8},{10,9},{11,1... | collective-permute-start | bytes 20 | tf_op jit(solution)/shard_map/while/body/eval_jaxpr/ppermute | solution.py:15
  119.4 10.5 %collective-permute-start = (f32[1]{0:T(128)}, f32[1]{0:T(128)}, u32[]{:S(2)}, u32[]{:S(2)}) collective-permute-start(f32[1]{0:T(128)} %select_n.49), channel_id=1, source_target_pairs={{1,0},{2,1},{3,2},{4,3},{5,4},{6,5},{7,6},{8,7},{9,8},{10,9},{11,1... | collective-permute-start | bytes 20 | tf_op jit(solution)/shard_map/while/body/eval_jaxpr/ppermute | solution.py:15
  146.5 8.1 %collective-permute-start = (f32[1]{0:T(128)}, f32[1]{0:T(128)}, u32[]{:S(2)}, u32[]{:S(2)}) collective-permute-start(f32[1]{0:T(128)} %select_n.49), channel_id=1, source_target_pairs={{1,0},{2,1},{3,2},{4,3},{5,4},{6,5},{7,6},{8,7},{9,8},{10,9},{11,1... | collective-permute-start | bytes 20 | tf_op jit(solution)/shard_map/while/body/eval_jaxpr/ppermute | solution.py:15
  180.3 8.3 %collective-permute-start.1 = (f32[1]{0:T(128)}, f32[1]{0:T(128)}, u32[]{:S(2)}, u32[]{:S(2)}) collective-permute-start(f32[1]{0:T(128)} %select_n.51), channel_id=1, source_target_pairs={{1,0},{2,1},{3,2},{4,3},{5,4},{6,5},{7,6},{8,7},{9,8},{10,9},{11,1... | collective-permute-start | bytes 20 | tf_op jit(solution)/shard_map/while/body/eval_jaxpr/ppermute | solution.py:15
  192.2 11.7 %collective-permute-start.1 = (f32[1]{0:T(128)}, f32[1]{0:T(128)}, u32[]{:S(2)}, u32[]{:S(2)}) collective-permute-start(f32[1]{0:T(128)} %select_n.51), channel_id=1, source_target_pairs={{1,0},{2,1},{3,2},{4,3},{5,4},{6,5},{7,6},{8,7},{9,8},{10,9},{11,1... | collective-permute-start | bytes 20 | tf_op jit(solution)/shard_map/while/body/eval_jaxpr/ppermute | solution.py:15
  195.0 9.0 %collective-permute-start = (f32[1]{0:T(128)}, f32[1]{0:T(128)}, u32[]{:S(2)}, u32[]{:S(2)}) collective-permute-start(f32[1]{0:T(128)} %select_n.49), channel_id=1, source_target_pairs={{1,0},{2,1},{3,2},{4,3},{5,4},{6,5},{7,6},{8,7},{9,8},{10,9},{11,1... | collective-permute-start | bytes 20 | tf_op jit(solution)/shard_map/while/body/eval_jaxpr/ppermute | solution.py:15
  206.0 13.2 %collective-permute-start.1 = (f32[1]{0:T(128)}, f32[1]{0:T(128)}, u32[]{:S(2)}, u32[]{:S(2)}) collective-permute-start(f32[1]{0:T(128)} %select_n.51), channel_id=1, source_target_pairs={{1,0},{2,1},{3,2},{4,3},{5,4},{6,5},{7,6},{8,7},{9,8},{10,9},{11,1... | collective-permute-start | bytes 20 | tf_op jit(solution)/shard_map/while/body/eval_jaxpr/ppermute | solution.py:15
  208.8 10.5 %collective-permute-start = (f32[1]{0:T(128)}, f32[1]{0:T(128)}, u32[]{:S(2)}, u32[]{:S(2)}) collective-permute-start(f32[1]{0:T(128)} %select_n.49), channel_id=1, source_target_pairs={{1,0},{2,1},{3,2},{4,3},{5,4},{6,5},{7,6},{8,7},{9,8},{10,9},{11,1... | collective-permute-start | bytes 20 | tf_op jit(solution)/shard_map/while/body/eval_jaxpr/ppermute | solution.py:15
  221.2 13.2 %collective-permute-start.1 = (f32[1]{0:T(128)}, f32[1]{0:T(128)}, u32[]{:S(2)}, u32[]{:S(2)}) collective-permute-start(f32[1]{0:T(128)} %select_n.51), channel_id=1, source_target_pairs={{1,0},{2,1},{3,2},{4,3},{5,4},{6,5},{7,6},{8,7},{9,8},{10,9},{11,1... | collective-permute-start | bytes 20 | tf_op jit(solution)/shard_map/while/body/eval_jaxpr/ppermute | solution.py:15
  224.1 10.4 %collective-permute-start = (f32[1]{0:T(128)}, f32[1]{0:T(128)}, u32[]{:S(2)}, u32[]{:S(2)}) collective-permute-start(f32[1]{0:T(128)} %select_n.49), channel_id=1, source_target_pairs={{1,0},{2,1},{3,2},{4,3},{5,4},{6,5},{7,6},{8,7},{9,8},{10,9},{11,1... | collective-permute-start | bytes 20 | tf_op jit(solution)/shard_map/while/body/eval_jaxpr/ppermute | solution.py:15
  236.4 13.1 %collective-permute-start.1 = (f32[1]{0:T(128)}, f32[1]{0:T(128)}, u32[]{:S(2)}, u32[]{:S(2)}) collective-permute-start(f32[1]{0:T(128)} %select_n.51), channel_id=1, source_target_pairs={{1,0},{2,1},{3,2},{4,3},{5,4},{6,5},{7,6},{8,7},{9,8},{10,9},{11,1... | collective-permute-start | bytes 20 | tf_op jit(solution)/shard_map/while/body/eval_jaxpr/ppermute | solution.py:15
  239.3 10.3 %collective-permute-start = (f32[1]{0:T(128)}, f32[1]{0:T(128)}, u32[]{:S(2)}, u32[]{:S(2)}) collective-permute-start(f32[1]{0:T(128)} %select_n.49), channel_id=1, source_target_pairs={{1,0},{2,1},{3,2},{4,3},{5,4},{6,5},{7,6},{8,7},{9,8},{10,9},{11,1... | collective-permute-start | bytes 20 | tf_op jit(solution)/shard_map/while/body/eval_jaxpr/ppermute | solution.py:15
  251.5 13.2 %collective-permute-start.1 = (f32[1]{0:T(128)}, f32[1]{0:T(128)}, u32[]{:S(2)}, u32[]{:S(2)}) collective-permute-start(f32[1]{0:T(128)} %select_n.51), channel_id=1, source_target_pairs={{1,0},{2,1},{3,2},{4,3},{5,4},{6,5},{7,6},{8,7},{9,8},{10,9},{11,1... | collective-permute-start | bytes 20 | tf_op jit(solution)/shard_map/while/body/eval_jaxpr/ppermute | solution.py:15
  254.4 10.5 %collective-permute-start = (f32[1]{0:T(128)}, f32[1]{0:T(128)}, u32[]{:S(2)}, u32[]{:S(2)}) collective-permute-start(f32[1]{0:T(128)} %select_n.49), channel_id=1, source_target_pairs={{1,0},{2,1},{3,2},{4,3},{5,4},{6,5},{7,6},{8,7},{9,8},{10,9},{11,1... | collective-permute-start | bytes 20 | tf_op jit(solution)/shard_map/while/body/eval_jaxpr/ppermute | solution.py:15
  266.8 13.2 %collective-permute-start.1 = (f32[1]{0:T(128)}, f32[1]{0:T(128)}, u32[]{:S(2)}, u32[]{:S(2)}) collective-permute-start(f32[1]{0:T(128)} %select_n.51), channel_id=1, source_target_pairs={{1,0},{2,1},{3,2},{4,3},{5,4},{6,5},{7,6},{8,7},{9,8},{10,9},{11,1... | collective-permute-start | bytes 20 | tf_op jit(solution)/shard_map/while/body/eval_jaxpr/ppermute | solution.py:15
  269.6 10.5 %collective-permute-start = (f32[1]{0:T(128)}, f32[1]{0:T(128)}, u32[]{:S(2)}, u32[]{:S(2)}) collective-permute-start(f32[1]{0:T(128)} %select_n.49), channel_id=1, source_target_pairs={{1,0},{2,1},{3,2},{4,3},{5,4},{6,5},{7,6},{8,7},{9,8},{10,9},{11,1... | collective-permute-start | bytes 20 | tf_op jit(solution)/shard_map/while/body/eval_jaxpr/ppermute | solution.py:15
  282.0 13.2 %collective-permute-start.1 = (f32[1]{0:T(128)}, f32[1]{0:T(128)}, u32[]{:S(2)}, u32[]{:S(2)}) collective-permute-start(f32[1]{0:T(128)} %select_n.51), channel_id=1, source_target_pairs={{1,0},{2,1},{3,2},{4,3},{5,4},{6,5},{7,6},{8,7},{9,8},{10,9},{11,1... | collective-permute-start | bytes 20 | tf_op jit(solution)/shard_map/while/body/eval_jaxpr/ppermute | solution.py:15
  284.9 10.4 %collective-permute-start = (f32[1]{0:T(128)}, f32[1]{0:T(128)}, u32[]{:S(2)}, u32[]{:S(2)}) collective-permute-start(f32[1]{0:T(128)} %select_n.49), channel_id=1, source_target_pairs={{1,0},{2,1},{3,2},{4,3},{5,4},{6,5},{7,6},{8,7},{9,8},{10,9},{11,1... | collective-permute-start | bytes 20 | tf_op jit(solution)/shard_map/while/body/eval_jaxpr/ppermute | solution.py:15
  300.1 12.4 %collective-permute-start = (f32[1]{0:T(128)}, f32[1]{0:T(128)}, u32[]{:S(2)}, u32[]{:S(2)}) collective-permute-start(f32[1]{0:T(128)} %select_n.49), channel_id=1, source_target_pairs={{1,0},{2,1},{3,2},{4,3},{5,4},{6,5},{7,6},{8,7},{9,8},{10,9},{11,1... | collective-permute-start | bytes 20 | tf_op jit(solution)/shard_map/while/body/eval_jaxpr/ppermute | solution.py:15
  317.2 10.5 %collective-permute-start = (f32[1]{0:T(128)}, f32[1]{0:T(128)}, u32[]{:S(2)}, u32[]{:S(2)}) collective-permute-start(f32[1]{0:T(128)} %select_n.49), channel_id=1, source_target_pairs={{1,0},{2,1},{3,2},{4,3},{5,4},{6,5},{7,6},{8,7},{9,8},{10,9},{11,1... | collective-permute-start | bytes 20 | tf_op jit(solution)/shard_map/while/body/eval_jaxpr/ppermute | solution.py:15
  332.5 10.5 %collective-permute-start = (f32[1]{0:T(128)}, f32[1]{0:T(128)}, u32[]{:S(2)}, u32[]{:S(2)}) collective-permute-start(f32[1]{0:T(128)} %select_n.49), channel_id=1, source_target_pairs={{1,0},{2,1},{3,2},{4,3},{5,4},{6,5},{7,6},{8,7},{9,8},{10,9},{11,1... | collective-permute-start | bytes 20 | tf_op jit(solution)/shard_map/while/body/eval_jaxpr/ppermute | solution.py:15
  347.7 10.4 %collective-permute-start = (f32[1]{0:T(128)}, f32[1]{0:T(128)}, u32[]{:S(2)}, u32[]{:S(2)}) collective-permute-start(f32[1]{0:T(128)} %select_n.49), channel_id=1, source_target_pairs={{1,0},{2,1},{3,2},{4,3},{5,4},{6,5},{7,6},{8,7},{9,8},{10,9},{11,1... | collective-permute-start | bytes 20 | tf_op jit(solution)/shard_map/while/body/eval_jaxpr/ppermute | solution.py:15
  (42 other events, 362.3 us)
Sparse Core Ops, SparseCore 0:
  10.8 358.9 all-gather.1
where the time goes:
time: 505 us; the launch traced here: 503 us
  waiting for transfers between devices  186 us (37%)
  starting transfers between devices  174 us (34%)
  matrix products  61.7 us (12%)
  loops' own time  59.6 us (12%)
  between operations  15.4 us (3%)
    ppermute x62, waiting for transfers between devices, from_behind(): return lax.ppermute(shard, axis, pairs)  185 us
    ppermute x62, starting transfers between devices, from_behind(): return lax.ppermute(shard, axis, pairs)  174 us
    another operation x1, loops' own time, doc_returns(): beyond = lax.fori_loop(0, lax.axis_size('seq') - 1, advance, blank)  59.6 us
    dot_general x1, matrix products, body(): lax.dot_general(grad_resid, down_full, (((1,), (1,)), ((), ())), preferre...  32.6 us
    dot_general x1, matrix products, body(): jnp.dot(hidden, down_full, preferred_element_type=jnp.float32)  28.1 us
  transfers between devices with their start and end apart: 63, of which 62 were waited for; matrix products, arithmetic and copies ran while one was open for 1% of the time, Pallas kernels for 0%

commit v1 on v0

v1 whole, which is shorter than its diff:
```python
import functools
import jax
import jax.numpy as jnp
from jax import lax
from jax.experimental import pallas as pl
from jax.experimental.pallas import tpu as pltpu
from jax.sharding import PartitionSpec as P

EPS = 1e-06
LANES = 128
CHUNKS = (("plane", "y", 3), ("plane", "x", 3), ("ring", "y", 6), ("ring", "x", 6), ("ring", "y", 5), ("ring", "x", 5))


def chunk_columns(width):
    tiles = width // LANES
    shares = sum(share for _, _, share in CHUNKS)
    edges, done = [0], 0
    for _, _, share in CHUNKS:
        done += share
        edges.append((tiles * done // shares) * LANES)
    edges[-1] = width
    return [(edges[k], edges[k + 1] - edges[k]) for k in range(len(CHUNKS))]


def gather_multiply(columns, hidden_ref, w_ref, full_ref, acc_ref, slots,
                    send_x, send_y, send_up, send_down, send_core, recv, core_recv, slot_sem, own_sem):
    me = lax.axis_index("seq")
    core = lax.rem(me, 2)
    x = lax.rem(lax.div(me, 2), 2)
    y = lax.rem(lax.div(me, 4), 2)
    z = lax.div(me, 8)
    other_core = me + 1 - 2 * core
    at_x = me + 2 - 4 * x
    at_y = me + 4 - 8 * y
    above = me + 8
    below = me - 8
    is_end = 1 - lax.div(z * (3 - z), 2)
    toward = 1 - 2 * lax.div(z, 2)

    def plane_of(turn):
        odd = lax.rem(turn, 2)
        zigzag = odd * lax.div(turn + 1, 2) - (1 - odd) * lax.div(turn, 2)
        return z + toward * (is_end * turn + (1 - is_end) * zigzag)

    def chip_of(dx, dy, turn):
        sx = x + dx - 2 * dx * x
        sy = y + dy - 2 * dy * y
        return plane_of(turn) * 4 + sy * 2 + sx

    def remote(k, src, chip, sends, recvs, target):
        start, size = columns[k]
        shard = 2 * chip + core
        where = full_ref.at[shard, :, pl.ds(start, size)]
        source = where if src is None else src.at[:, pl.ds(start, size)]
        return pltpu.make_async_remote_copy(
            src_ref=source, dst_ref=where, send_sem=sends.at[chip, k], recv_sem=recvs.at[chip, k],
            device_id={"seq": target}, device_id_type=pl.DeviceIdType.MESH)

    def onward(k, dx, dy, turn, act, src=None):
        kind, via, _ = CHUNKS[k]
        chip = chip_of(dx, dy, turn)
        come_from = plane_of(turn)

        def z_copies():
            @pl.when(jnp.logical_and(come_from >= z, z > 0))
            def _():
                act(remote(k, src, chip, send_down, recv, below))

            @pl.when(jnp.logical_and(come_from <= z, z < 3))
            def _():
                act(remote(k, src, chip, send_up, recv, above))

        def plane_copies():
            if dx == 0 and (dy == 0 or via == "x"):
                act(remote(k, src, chip, send_x, recv, at_x))
            if dy == 0 and (dx == 0 or via == "y"):
                act(remote(k, src, chip, send_y, recv, at_y))

        if kind == "ring":
            if dx == 0 and dy == 0:
                z_copies()
            plane_copies()
        else:
            z_copies()

            @pl.when(turn == 0)
            def _():
                plane_copies()
        act(remote(k, src, chip, send_core, core_recv, other_core))

    def arrived(k, dx, dy, turn, recvs):
        chip = chip_of(dx, dy, turn)
        remote(k, None, chip, send_x, recvs, at_x).wait_recv()

    start_it = lambda copy: copy.start()
    wait_it = lambda copy: copy.wait_send()

    barrier = pltpu.get_barrier_semaphore()
    for target in (other_core, at_x, at_y):
        pl.semaphore_signal(barrier, inc=1, device_id={"seq": target}, device_id_type=pl.DeviceIdType.MESH)

    @pl.when(z > 0)
    def _():
        pl.semaphore_signal(barrier, inc=1, device_id={"seq": below}, device_id_type=pl.DeviceIdType.MESH)

    @pl.when(z < 3)
    def _():
        pl.semaphore_signal(barrier, inc=1, device_id={"seq": above}, device_id_type=pl.DeviceIdType.MESH)

    pl.semaphore_wait(barrier, 5 - is_end)

    zero = me * 0
    for k in range(len(columns)):
        onward(k, 0, 0, zero, start_it, w_ref)
    own = pltpu.make_async_copy(w_ref, full_ref.at[me], own_sem)
    own.start()
    acc_ref[...] = jnp.zeros_like(acc_ref)
    own.wait()

    def for_pieces(turn_now, fn):
        def one(t, carry):
            dx = lax.rem(t, 2)
            dy = lax.div(t, 2)
            turn = turn_now - 1 - dx - dy

            @pl.when(jnp.logical_and(turn >= 0, turn <= 3))
            def _():
                fn(t, dx, dy, turn)
            return carry
        lax.fori_loop(0, 4, one, 0)

    def slot_copy(k, t, chip, side):
        start, size = columns[k]
        shard = 2 * chip + (core if side == 0 else 1 - core)
        return pltpu.make_async_copy(
            full_ref.at[shard, :, pl.ds(start, size)], slots.at[2 * t + side, :, pl.ds(0, size)],
            slot_sem.at[2 * t + side])

    def step(turn_now, carry):
        for k in range(len(columns)):
            start, size = columns[k]

            def bring(t, dx, dy, turn):
                arrived(k, dx, dy, turn, core_recv)
                chip = chip_of(dx, dy, turn)
                slot_copy(k, t, chip, 0).start()
                slot_copy(k, t, chip, 1).start()
            for_pieces(turn_now, bring)

            @pl.when(turn_now <= 3)
            def _():
                arrived(k, 0, 0, turn_now, recv)
                onward(k, 0, 0, turn_now, start_it)

            @pl.when(turn_now <= 4)
            def _():
                for dx, dy in ((1, 0), (0, 1)):
                    arrived(k, dx, dy, turn_now - 1, recv)
                    onward(k, dx, dy, turn_now - 1, start_it)

            @pl.when(jnp.logical_and(turn_now >= 2, turn_now <= 5))
            def _():
                arrived(k, 1, 1, turn_now - 2, recv)
                onward(k, 1, 1, turn_now - 2, start_it)

            def multiply(t, dx, dy, turn):
                chip = chip_of(dx, dy, turn)
                slot_copy(k, t, chip, 0).wait()
                slot_copy(k, t, chip, 1).wait()
                near = jnp.dot(hidden_ref[2 * chip + core], slots[2 * t, :, :size],
                               preferred_element_type=jnp.float32)
                far = jnp.dot(hidden_ref[2 * chip + 1 - core], slots[2 * t + 1, :, :size],
                              preferred_element_type=jnp.float32)
                acc_ref[:, start:start + size] += near + far
            for_pieces(turn_now, multiply)
        return carry

    lax.fori_loop(1, 7, step, 0)

    for k in range(len(columns)):
        onward(k, 0, 0, zero, wait_it, w_ref)

    def drain(turn, carry):
        for k in range(len(columns)):
            @pl.when(turn >= 1)
            def _():
                onward(k, 0, 0, turn, wait_it)
            for dx, dy in ((1, 0), (0, 1), (1, 1)):
                onward(k, dx, dy, turn, wait_it)
        return carry

    lax.fori_loop(0, 4, drain, 0)


def gather_and_project(hidden_blocks, weight):
    devices, rows, depth = hidden_blocks.shape
    width = weight.shape[1]
    columns = chunk_columns(width)
    chips = devices // 2
    sems = pltpu.SemaphoreType.DMA((chips, len(columns)))
    return pl.pallas_call(
        functools.partial(gather_multiply, columns),
        out_shape=(
            jax.ShapeDtypeStruct((devices, depth, width), weight.dtype),
            jax.ShapeDtypeStruct((rows, width), jnp.float32),
        ),
        in_specs=[pl.BlockSpec(memory_space=pltpu.VMEM), pl.BlockSpec(memory_space=pl.ANY)],
        out_specs=(pl.BlockSpec(memory_space=pl.ANY), pl.BlockSpec(memory_space=pltpu.VMEM)),
        scratch_shapes=[
            pltpu.VMEM((8, depth, max(size for _, size in columns)), weight.dtype),
            sems, sems, sems, sems, sems, sems, sems,
            pltpu.SemaphoreType.DMA((8,)),
            pltpu.SemaphoreType.DMA(()),
        ],
        compiler_params=pltpu.CompilerParams(
            collective_id=0, has_side_effects=True, vmem_limit_bytes=40 * 1024 * 1024),
        cost_estimate=pl.CostEstimate(
            flops=2 * rows * devices * depth * width,
            bytes_accessed=3 * devices * depth * width * 2, transcendentals=0),
    )(hidden_blocks, weight)


def doc_returns(rewards, seg_ids):
    count = rewards.shape[0]
    first_id = seg_ids[0]
    last_id = seg_ids[count - 1]
    first_total = jnp.sum(jnp.where(seg_ids == first_id, rewards, 0.0))
    own = jnp.stack([first_id.astype(jnp.float32), first_total])
    every = lax.all_gather(own, "seq", axis=0)
    places = lax.broadcasted_iota(jnp.int32, (count, count), 0)
    others = lax.broadcasted_iota(jnp.int32, (count, count), 1)
    same_doc = seg_ids[:, None] == seg_ids[None, :]
    suffix = jnp.logical_and(same_doc, others >= places)
    local_sum = jnp.sum(jnp.where(suffix, rewards[None, :], 0.0), axis=1)
    later = jnp.arange(every.shape[0]) > lax.axis_index("seq")
    joined = jnp.logical_and(later, every[:, 0] == last_id.astype(jnp.float32))
    carried = jnp.sum(jnp.where(joined, every[:, 1], 0.0))
    return local_sum + jnp.where(seg_ids == last_id, carried, 0.0)


def body(in_kernel, resid, gate_pre, up_pre, down_weight, norm_gain, value_head, rewards, seg_ids):
    gate = gate_pre.astype(jnp.float32)
    upval = up_pre.astype(jnp.float32)
    sigma = jax.nn.sigmoid(gate)
    active = gate * sigma
    hidden = (active * upval).astype(jnp.bfloat16)
    returns = doc_returns(rewards, seg_ids)
    if in_kernel:
        rows, depth = hidden.shape[0], down_weight.shape[0]
        blocks = hidden.reshape(rows, hidden.shape[1] // depth, depth).transpose(1, 0, 2)
        down_full, product = gather_and_project(blocks, down_weight)
        down_full = down_full.reshape(hidden.shape[1], down_weight.shape[1])
    else:
        down_full = lax.all_gather(down_weight, "seq", axis=0, tiled=True)
        partial_value = jnp.dot(hidden, down_full, preferred_element_type=jnp.float32)
        product = lax.psum(partial_value, "tp")
    head = norm_gain * value_head
    stream = resid.astype(jnp.float32) + product
    width = stream.shape[1]
    rinv = lax.rsqrt(jnp.mean(stream * stream, axis=1) + EPS)
    values = jnp.sum(stream * head[None, :], axis=1) * rinv
    grad_value = 64.0 * (values - returns)
    grad_stream = (grad_value * rinv)[:, None] * (
        head[None, :] - stream * (rinv * values / width)[:, None]
    )
    grad_resid = grad_stream.astype(jnp.bfloat16)
    grad_hidden = lax.dot_general(
        grad_resid, down_full, (((1,), (1,)), ((), ())), preferred_element_type=jnp.float32
    )
    grad_gate = (grad_hidden * upval * sigma * (1.0 + gate * (1.0 - sigma))).astype(jnp.bfloat16)
    grad_up = (grad_hidden * active).astype(jnp.bfloat16)
    advantages = returns - values
    return (values, advantages, grad_gate, grad_up, grad_resid)


def solution(mesh):
    in_kernel = mesh.shape["groups"] == 1 and mesh.shape["tp"] == 1 and mesh.shape["seq"] == 32
    return jax.shard_map(
        functools.partial(body, in_kernel),
        mesh=mesh,
        in_specs=(
            P(("groups", "seq"), None),
            P(("groups", "seq"), "tp"),
            P(("groups", "seq"), "tp"),
            P(("tp", "seq"), None),
            P(),
            P(),
            P(("groups", "seq")),
            P(("groups", "seq")),
        ),
        out_specs=(
            P(("groups", "seq")),
            P(("groups", "seq")),
            P(("groups", "seq"), "tp"),
            P(("groups", "seq"), "tp"),
            P(("groups", "seq"), None),
        ),
        check_vma=False,
    )
```

time: 505 us -> 377 us (0.75)
  the two profiles are of different devices: /device:TPU:15 before, /device:TPU:0 now
where the time goes in v1:
time: 377 us; the launch traced here: 376 us
  Pallas kernels  267 us (71%)
  blocking collectives  42 us (11%)
  matrix products  32.5 us (9%)
  local copies, waits for them, and re-layouts  17.8 us (5%)
  other arithmetic  15 us (4%)
    pallas_call x1, Pallas kernels, gather_and_project(): pl.pallas_call(functools.partial(gather_multiply, columns), out_shape=(ja...  267 us
    unnamed x1, blocking collectives  42 us
    dot_general x1, matrix products, body(): lax.dot_general(grad_resid, down_full, (((1,), (1,)), ((), ())), preferre...  32.5 us
    reshape x2, local copies, waits for them, and re-layouts, body(): hidden.reshape(rows, hidden.shape[1] // depth, depth).transpose(1, 0, 2)  16.2 us

profile of v1, /device:TPU:0, one launch (start us, length us, event | category | flops | bytes accessed | tf_op | source)
XLA Modules:
  0.0 376.2 jit_solution(15041153172750186881)
XLA Ops:
  0.6 0.9 select_reduce_fusion
  1.6 1.3 fusion.16
  2.9 1.9 fusion.11
  6.2 0.8 maximum_dynamic-update-slice_fusion
  7.0 42.0 %all-reduce = f32[64]{0:T(128)S(1)} all-reduce(f32[64]{0:T(128)S(1)} %maximum_dynamic-update-slice_fusion), channel_id=2, replica_groups=mesh['groups'=1,'seq'=32,'tp'=1] {'seq'}, use_global_device_ids=true, to_apply=%add | all-reduce | flops 64 | bytes 512
  49.0 0.1 reshape.35
  49.1 0.1 fusion.9
  49.2 0.2 slice_reduce_fusion
  49.4 0.6 fusion.12
  50.0 0.7 mul.76
  50.7 5.4 %fusion = bf16[192,9472]{1,0:T(8,128)(2,1)} fusion(bf16[192,9472]{1,0:T(8,128)(2,1)} %param.10, bf16[192,9472]{1,0:T(8,128)(2,1)} %param.9), kind=kLoop, calls=%fused_computation.5 | loop fusion | flops 14548992 | bytes 10911744 | tf_op jit(solution)/shard_map/convert_element_type | solution.py:246
  56.1 12.0 %reshape.33 = bf16[192,32,296]{2,1,0:T(8,128)(2,1)} reshape(bf16[192,9472]{1,0:T(8,128)(2,1)} %fusion) | data formatting | bytes 7274496 | tf_op jit(solution)/shard_map/reshape | solution.py:250
  68.1 4.2 %copy.16 = bf16[192,32,296]{2,0,1:T(8,128)(2,1)S(1)} copy(bf16[192,32,296]{2,1,0:T(8,128)(2,1)} %reshape.33) | data formatting | bytes 7274496 | tf_op jit(solution)/shard_map/reshape | solution.py:250
  72.3 0.0 copy-start.1
  72.3 266.6 %shard_map.119 = (bf16[32,296,3584]{2,1,0:T(8,128)(2,1)}, f32[192,3584]{1,0:T(8,128)S(1)}) custom-call(bf16[32,192,296]{2,1,0:T(8,128)(2,1)S(1)} %bitcast.10, bf16[296,3584]{1,0:T(8,128)(2,1)S(1)} %copy-done), custom_call_target="tpu_custom_call" | custom-call | flops 13035896832 | bytes 203685888 | tf_op jit(solution)/shard_map/pallas_call | solution.py:201
  339.0 0.0 copy-start.3
  339.0 0.6 multiply_reduce_fusion
  339.7 0.0 copy-done.3
  339.7 1.3 multiply_multiply_fusion.1
  341.0 0.0 copy-start.4
  341.0 1.9 multiply_multiply_fusion
  342.9 0.6 multiply_convert_fusion.1
  343.5 0.0 copy-start.2
  343.5 32.5 %multiply_convert_fusion = (bf16[192,9472]{1,0:T(8,128)(2,1)}, bf16[192,9472]{1,0:T(8,128)(2,1)}) fusion(bf16[192,9472]{1,0:T(8,128)(2,1)} %param.9, bf16[192,9472]{1,0:T(8,128)(2,1)} %param.10, bf16[192,3584]{1,0:T(8,128)(2,1)S(1)} %multiply_convert_fusion.1, bf16[9472,3584]{1,0:T(8,128)(2,1)} %bitcast.5), kind=kOutput, calls=%fused_computation.13 | convolution fusion | flops 13063176192 | bytes 83820544 | tf_op jit(solution)/shard_map/dot_general | solution.py:267
  (6 shorter events, 0.0 us)
Async XLA Ops:
  68.1 4.2 %copy-start = (bf16[296,3584]{1,0:T(8,128)(2,1)S(1)}, bf16[296,3584]{1,0:T(8,128)(2,1)}, u32[]{:S(2)}) copy-start(bf16[296,3584]{1,0:T(8,128)(2,1)} %w_ref.1) | copy-start | bytes 6365188
  72.3 266.7 %copy-start.1 = (bf16[192,3584]{1,0:T(8,128)(2,1)S(1)}, bf16[192,3584]{1,0:T(8,128)(2,1)}, u32[]{:S(2)}) copy-start(bf16[192,3584]{1,0:T(8,128)(2,1)} %param.8) | copy-start | bytes 4128772
  339.0 0.7 copy-start.3
  341.0 35.0 %copy-start.4 = (f32[192]{0:T(256)}, f32[192]{0:T(256)S(1)}, u32[]{:S(2)}) copy-start(f32[192]{0:T(256)S(1)} %get-tuple-element.12) | copy-start | bytes 2308
  343.5 32.5 %copy-start.2 = (bf16[192,3584]{1,0:T(8,128)(2,1)}, bf16[192,3584]{1,0:T(8,128)(2,1)S(1)}, u32[]{:S(2)}) copy-start(bf16[192,3584]{1,0:T(8,128)(2,1)S(1)} %multiply_convert_fusion.1) | copy-start | bytes 4128772
